TPU v7x, 32 devices: a whole 2x2x4 slice. The times are simulated.
32 devices in a mesh: ctx: 8 (over y, x, core), head: 4 (over z).
Axes of the slice: x: 2, y: 2, z: 4, core: 2. Of those that a mesh axis runs over, the one named last changes fastest.
Arguments:
- queries: bfloat16 [2048, 2560], P('ctx', 'head'), may hold values from -6 to 6
- keys: bfloat16 [2048, 2560], P('ctx', 'head'), may hold values from -6 to 6
- values: bfloat16 [2048, 2560], P('ctx', 'head'), may hold values from -16 to 16
- out_weight: bfloat16 [2560, 2560], P('head'), may hold values from -0.125 to 0.125
- cotangent: bfloat16 [2048, 2560], P('ctx', 'head'), may hold values from -16 to 16
- contacts: int32 [16, 16], replicated, may hold values 0 or 1
- chains: int32 [16], replicated, may hold values from 0 to 3, never falling along the last dimension, each value on 1 to 8 neighbouring positions
Outputs:
- mixed: bfloat16 [2048, 2560], P('ctx', 'head')
- query_grad: bfloat16 [2048, 2560], P('ctx', 'head')
- key_grad: bfloat16 [2048, 2560], P('ctx', 'head')
- value_grad: bfloat16 [2048, 2560], P('ctx', 'head')
Inputs may be any that keep to these rules, and one draw needn't show every extreme that they name: `chains`: chain numbers never fall along the blocks; each chain has 1 to 8 blocks, one exactly 8.
All inputs are finite; a program needn't handle non-finite values.
Results may differ from a plain program's by a relative error of at most 0.02.
Values may be sent and summed in bfloat16 or wider, within the bound.
A program may use at most 192 MiB of HBM per device.

v0:
```python
import jax
import jax.numpy as jnp
from jax import lax
from jax.sharding import PartitionSpec as P

HEAD_SIZE = 128
BLOCK = 128


NEG = -1e30


def rounded(value):
    return lax.optimization_barrier(value.astype(jnp.bfloat16)).astype(jnp.float32)


def block_mask(allowed, row_start, col_start, row_count, col_count):
    part_mask = lax.dynamic_slice(
        allowed, (row_start // BLOCK, col_start // BLOCK), (row_count // BLOCK, col_count // BLOCK)
    )
    part_mask = jnp.repeat(jnp.repeat(part_mask, BLOCK, axis=0), BLOCK, axis=1)
    return part_mask[:, None, :]


def forward_fold(q_three, allowed, own_start):
    scale = HEAD_SIZE ** (-0.5)
    rows, heads, size = q_three.shape

    def step(carry, piece, start):
        best, total, accum = carry
        key_rows, value_rows = piece
        count = key_rows.shape[0]
        k_three = key_rows.reshape(count, heads, size)
        v_three = value_rows.reshape(count, heads, size)
        scores = (
            jnp.einsum("qhd,khd->qhk", q_three, k_three, preferred_element_type=jnp.float32) * scale
        )
        keep = block_mask(allowed, own_start, start, rows, count)
        scores = jnp.where(keep, scores, NEG)
        best_new = jnp.maximum(best, jnp.max(scores, axis=2))
        weights = jnp.where(keep, jnp.exp(scores - best_new[:, :, None]), 0.0)
        total = jnp.sum(weights, axis=2)
        accum = jnp.einsum(
            "qhk,khd->qhd",
            weights.astype(jnp.bfloat16),
            v_three,
            preferred_element_type=jnp.float32,
        )
        return (best_new, total, accum)

    return step


def key_fold(q_three, g_three, lse, delta, allowed, own_start):
    scale = HEAD_SIZE ** (-0.5)
    rows, heads, size = q_three.shape

    def step(carry, piece, start):
        key_rows, value_rows = piece
        count = key_rows.shape[0]
        groups = count // rows
        k_three = key_rows.reshape(count, heads, size)
        v_three = value_rows.reshape(count, heads, size)
        scores = (
            jnp.einsum("qhd,khd->qhk", q_three, k_three, preferred_element_type=jnp.float32) * scale
        )
        keep = block_mask(allowed, own_start, start, rows, count)
        probs = jnp.where(keep, jnp.exp(scores - lse[:, :, None]), 0.0)
        dprob = jnp.einsum("qhd,khd->qhk", g_three, v_three, preferred_element_type=jnp.float32)
        dscore = (probs * (dprob - delta[:, :, None])).astype(jnp.bfloat16)
        q_parts = (
            jnp.einsum(
                "qhgk,gkhd->gqhd",
                dscore.reshape(rows, heads, groups, rows),
                k_three.reshape(groups, rows, heads, size),
                preferred_element_type=jnp.float32,
            )
            * scale
        )
        q_accum = jnp.sum(rounded(q_parts), axis=0)
        key_part = (
            jnp.einsum("qhk,qhd->khd", dscore, q_three, preferred_element_type=jnp.float32) * scale
        ).astype(jnp.bfloat16)
        value_part = jnp.einsum(
            "qhk,qhd->khd", probs.astype(jnp.bfloat16), g_three, preferred_element_type=jnp.float32
        ).astype(jnp.bfloat16)
        key_term = key_part.reshape(count, heads * size)
        value_term = value_part.reshape(count, heads * size)
        return (q_accum, key_term, value_term)

    return step


def per_device(queries, keys, values, out_weight, cotangent, contacts, chains):
    rows = queries.shape[0]
    size = HEAD_SIZE
    heads = queries.shape[1] // size
    width = heads * size
    length = rows * lax.axis_size("ctx")
    allowed = jnp.logical_or(chains[:, None] == chains[None, :], contacts > 0)
    own_start = lax.axis_index("ctx") * rows
    q_three = queries.reshape(rows, heads, size)
    init = (
        jnp.full((rows, heads), NEG, jnp.float32),
        jnp.zeros((rows, heads), jnp.float32),
        jnp.zeros((rows, heads, size), jnp.float32),
    )
    forward_step = forward_fold(q_three, allowed, own_start)
    best, total, accum = forward_step(
        init,
        (
            lax.all_gather(keys, "ctx", axis=0, tiled=True),
            lax.all_gather(values, "ctx", axis=0, tiled=True),
        ),
        jnp.int32(0),
    )
    attended = (accum / total[:, :, None]).astype(jnp.bfloat16)
    lse = best + jnp.log(total)
    projected = jnp.dot(
        attended.reshape(rows, width), out_weight, preferred_element_type=jnp.float32
    )
    mixed = lax.psum_scatter(
        projected.astype(jnp.bfloat16), "head", scatter_dimension=1, tiled=True
    )
    full_cotangent = lax.all_gather(cotangent, "head", axis=1, tiled=True)
    grads = lax.dot_general(
        full_cotangent, out_weight, (((1,), (1,)), ((), ())), preferred_element_type=jnp.float32
    ).astype(jnp.bfloat16)
    g_three = grads.reshape(rows, heads, size)
    delta = jnp.sum(g_three.astype(jnp.float32) * attended.astype(jnp.float32), axis=2)
    start_carry = (
        jnp.zeros((rows, heads, size), jnp.float32),
        jnp.zeros((length, width), jnp.bfloat16),
        jnp.zeros((length, width), jnp.bfloat16),
    )
    step = key_fold(q_three, g_three, lse, delta, allowed, own_start)
    q_accum, key_term, value_term = step(
        start_carry,
        (
            lax.all_gather(keys, "ctx", axis=0, tiled=True),
            lax.all_gather(values, "ctx", axis=0, tiled=True),
        ),
        jnp.int32(0),
    )
    key_sum, value_sum = (
        lax.psum_scatter(
            key_term.astype(jnp.float32).astype(jnp.bfloat16),
            "ctx",
            scatter_dimension=0,
            tiled=True,
        ).astype(jnp.float32),
        lax.psum_scatter(
            value_term.astype(jnp.float32).astype(jnp.bfloat16),
            "ctx",
            scatter_dimension=0,
            tiled=True,
        ).astype(jnp.float32),
    )
    query_grad = q_accum.reshape(rows, width).astype(jnp.bfloat16)
    key_grad = key_sum.astype(jnp.bfloat16)
    value_grad = value_sum.astype(jnp.bfloat16)
    return (mixed, query_grad, key_grad, value_grad)


def solution(mesh):
    in_specs = (
        P("ctx", "head"),
        P("ctx", "head"),
        P("ctx", "head"),
        P("head", None),
        P("ctx", "head"),
        P(),
        P(),
    )
    out_specs = (P("ctx", "head"), P("ctx", "head"), P("ctx", "head"), P("ctx", "head"))
    return jax.shard_map(
        per_device, mesh=mesh, in_specs=in_specs, out_specs=out_specs, check_vma=False
    )
```

profile of v0, /device:TPU:0, one launch (start us, length us, event | category | flops | bytes accessed | tf_op | source)
XLA Modules:
  0.0 257.9 jit_solution(1913573517432876416)
XLA Ops:
  7.2 0.7 all-gather.8.cloned.1.call-update
  8.0 2.1 copy.44
  10.1 0.7 all-gather.6.cloned.1.call-update
  10.9 0.7 dynamic-slice
  11.6 0.8 compare_or_fusion
  12.6 1.9 copy.45
  14.4 30.2 %all-gather.8.cloned.1.call-done = bf16[256,2560]{1,0:T(8,128)(2,1)} async-done(((bf16[256,640]{1,0:T(8,128)(2,1)}), bf16[256,2560]{1,0:T(8,128)(2,1)}) %all-gather.8.cloned.1.call-update) | async-done | bytes 1310736 | tf_op jit(solution)/shard_map/all_gather | solution.py:125
  44.6 3.3 %convolution_convert_fusion.1 = bf16[256,640]{1,0:T(8,128)(2,1)} fusion(bf16[256,2560]{1,0:T(8,128)(2,1)} %all-gather.8.cloned.1.call-done, bf16[640,2560]{1,0:T(8,128)(2,1)S(1)} %copy-done), kind=kOutput, calls=%fused_computation.28 | convolution fusion | flops 839024640 | bytes 4915200 | tf_op jit(solution)/shard_map/dot_general | solution.py:126
  47.9 1.9 copy.50
  49.7 27.3 %all-gather.4.cloned.1.call-done = bf16[2048,640]{0,1:T(8,128)(2,1)} async-done(((bf16[256,640]{0,1:T(8,128)(2,1)}), bf16[2048,640]{0,1:T(8,128)(2,1)}) %all-gather.4.cloned.1.call-update) | async-done | bytes 2621456 | tf_op jit(solution)/shard_map/all_gather | solution.py:112
  77.2 4.1 %fusion.4 = (f32[256,5]{0,1:T(8,128)S(1)}, f32[5,2048,256]{2,1,0:T(8,128)S(1)}) fusion(pred[256,2048]{0,1:T(8,128)(4,1)S(1)} %bitcast.89, bf16[2048,5,128]{0,2,1:T(8,128)(2,1)} %bitcast.85, bf16[256,5,128]{0,2,1:T(8,128)(2,1)} %bitcast.94), kind=kOutput, calls=%fused_computation.8 | convolution fusion | flops 678951680 | bytes 13964288 | tf_op jit(solution)/shard_map/qhd,khd->qhk/dot_general | solution.py:36
  81.3 3.9 %copy-done.1 = f32[5,2048,256]{2,1,0:T(8,128)} copy-done((f32[5,2048,256]{2,1,0:T(8,128)}, f32[5,2048,256]{2,1,0:T(8,128)S(1)}, u32[]{:S(2)}) %copy-start.1) | copy-done | bytes 10485784
  85.2 2.5 fusion.6
  87.7 21.3 %all-gather.6.cloned.1.call-done = bf16[2048,640]{1,0:T(8,128)(2,1)} async-done(((bf16[256,640]{1,0:T(8,128)(2,1)}), bf16[2048,640]{1,0:T(8,128)(2,1)}) %all-gather.6.cloned.1.call-update) | async-done | bytes 2621456 | tf_op jit(solution)/shard_map/all_gather | solution.py:113
  109.1 4.5 %copy.48 = bf16[2048,640]{0,1:T(8,128)(2,1)} copy(bf16[2048,640]{1,0:T(8,128)(2,1)} %all-gather.6.cloned.1.call-done) | data formatting | bytes 5242880 | tf_op jit(solution)/shard_map/all_gather | solution.py:113
  113.6 7.7 %multiply_reduce_fusion = (f32[256,5]{0,1:T(8,128)S(1)}, bf16[256,5,128]{0,2,1:T(8,128)(2,1)S(1)}) fusion(bf16[256,5,128]{0,2,1:T(8,128)(2,1)} %bitcast.102, f32[256,5]{0,1:T(8,128)S(1)} %fusion.6, bf16[2048,5,128]{0,2,1:T(8,128)(2,1)} %bitcast.96, f32[5,2048,256]{2,1,0:T(8,128)} %copy-done.1, f32[256,5]{0,1:T(8,128)S(1)} %broadcast_maximum_fusion, ...), kind=kOutput, calls=%fused_computation.31 | convolution fusion | flops 685177600 | bytes 14302208 | tf_op jit(solution)/shard_map/qhk,khd->qhd/dot_general | solution.py:43
  121.3 2.3 convolution_convert_fusion
  123.5 2.4 copy.72
  126.3 8.0 %fusion.19 = bf16[5,128,2048]{2,1,0:T(8,128)(2,1)} fusion(bf16[256,5,128]{0,2,1:T(8,128)(2,1)} %bitcast.103, f32[5,2048,256]{2,1,0:T(8,128)} %copy-done.1, f32[256,5]{0,1:T(8,128)S(1)} %log_add_fusion, pred[256,2048]{0,1:T(8,128)(4,1)} %bitcast.92), kind=kOutput, calls=%fused_computation.24 | convolution fusion | flops 682885120 | bytes 13964288 | tf_op jit(solution)/shard_map/qhk,qhd->khd/dot_general | solution.py:84
  134.3 4.5 %copy.60 = bf16[2048,640]{1,0:T(8,128)(2,1)} copy(bf16[2048,640]{0,1:T(8,128)(2,1)} %bitcast.99) | data formatting | bytes 5242880 | tf_op jit(solution)/shard_map/reshape | solution.py:88
  138.8 8.5 %fusion.1 = bf16[256,5,2048]{0,2,1:T(8,128)(2,1)S(1)} fusion(f32[5,2048,256]{2,1,0:T(8,128)} %copy-done.1, f32[256,5]{0,1:T(8,128)S(1)} %get-tuple-element.14, f32[256,5]{0,1:T(8,128)S(1)} %log_add_fusion, pred[256,2048]{0,1:T(8,128)(4,1)} %bitcast.93, bf16[256,5,128]{0,2,1:T(8,128)(2,1)} %bitcast.104, bf16[2048,5,128]{0,2,1:T(8,128)(2,1)} %bitcast.97), kind=kOutput, calls=%fused_computation.2 | convolution fusion | flops 686817280 | bytes 19212288 | tf_op jit(solution)/shard_map/qhd,khd->qhk/dot_general | solution.py:69
  147.4 2.3 copy-done.2
  149.7 3.4 %multiply_convert_fusion = bf16[5,2048,128]{1,2,0:T(8,128)(2,1)} fusion(bf16[256,5,2048]{0,2,1:T(8,128)(2,1)S(1)} %fusion.1, bf16[256,5,128]{0,2,1:T(8,128)(2,1)S(1)} %bitcast.95), kind=kOutput, calls=%fused_computation.15 | convolution fusion | flops 673710080 | bytes 8192000 | tf_op jit(solution)/shard_map/qhk,qhd->khd/dot_general | solution.py:82
  153.1 4.4 %copy.58 = bf16[2048,640]{1,0:T(8,128)(2,1)} copy(bf16[2048,640]{0,1:T(8,128)(2,1)} %bitcast.84) | data formatting | bytes 5242880 | tf_op jit(solution)/shard_map/reshape | solution.py:87
  157.5 2.6 %copy.75 = bf16[80,8,8,256]{3,2,1,0:T(8,128)(2,1)S(1)} copy(bf16[80,8,8,256]{3,1,2,0:T(8,128)(2,1)} %bitcast.86) | data formatting | bytes 5242880
  160.1 6.1 %fusion.22 = bf16[8,256,5,128]{3,1,2,0:T(8,128)(2,1)} fusion(bf16[8,256,5,128]{1,0,3,2:T(8,128)(2,1)S(1)} %bitcast.98, bf16[256,5,8,256]{0,3,2,1:T(8,128)(2,1)} %bitcast.88), kind=kOutput, calls=%fused_computation.25 | convolution fusion | flops 673710080 | bytes 10485760 | tf_op jit(solution)/shard_map/qhgk,gkhd->gqhd/dot_general | solution.py:72
  166.3 3.2 %reduce_sum.32 = bf16[256,5,128]{2,0,1:T(8,128)(2,1)} reduce(bf16[8,256,5,128]{3,1,2,0:T(8,128)(2,1)} %fusion.22, bf16[]{:T(256)} %constant.51.clone.1), dimensions={0}, to_apply=%region_4.5 | reduce | flops 1146880 | bytes 2949122 | tf_op jit(solution)/shard_map/reduce_sum | solution.py:80
  169.4 1.9 copy.56
  171.3 1.9 copy.61
  173.2 1.9 copy.73
  175.0 28.6 %reduce-scatter.8.cloned.1.call-done = bf16[256,640]{1,0:T(8,128)(2,1)} async-done(((bf16[2048,640]{1,0:T(8,128)(2,1)}), bf16[256,640]{1,0:T(8,128)(2,1)}) %reduce-scatter.8.cloned.1.call-update) | async-done | bytes 327696 | tf_op jit(solution)/shard_map/reduce_scatter | solution.py:152
  203.6 47.4 %reduce-scatter.6.cloned.1.call-done = bf16[256,640]{1,0:T(8,128)(2,1)} async-done(((bf16[2048,640]{1,0:T(8,128)(2,1)}), bf16[256,640]{1,0:T(8,128)(2,1)}) %reduce-scatter.6.cloned.1.call-update) | async-done | bytes 327696 | tf_op jit(solution)/shard_map/reduce_scatter | solution.py:146
  (25 shorter events, 0.9 us)
Async XLA Ops:
  7.2 37.4 %copy-start = (bf16[640,2560]{1,0:T(8,128)(2,1)S(1)}, bf16[640,2560]{1,0:T(8,128)(2,1)}, u32[]{:S(2)}) copy-start(bf16[640,2560]{1,0:T(8,128)(2,1)} %param.10) | copy-start | bytes 9830404
  7.2 37.4 %all-gather.8.cloned.1.call-start = ((), (), s32[]{:S(2)}) async-start(), calls=%async_computation.5 | async-start | bytes 1638400 | tf_op jit(solution)/shard_map/all_gather | solution.py:125
  7.9 69.1 %all-gather.4.cloned.1.call-start = ((), (), s32[]{:S(2)}) async-start(), calls=%async_computation.3 | async-start | bytes 2949120 | tf_op jit(solution)/shard_map/all_gather | solution.py:112
  10.0 99.0 %all-gather.6.cloned.1.call-start = ((), (), s32[]{:S(2)}) async-start(), calls=%async_computation.4 | async-start | bytes 2949120 | tf_op jit(solution)/shard_map/all_gather | solution.py:113
  10.8 162.4 %reduce-scatter.10.cloned.1.call-start = ((), (), s32[]{:S(2)}) async-start(), calls=%async_computation.8 | async-start | bytes 1638400
  77.2 4.1 %copy-start.3 = (pred[256,16,128]{0,2,1:T(8,128)(4,1)}, pred[256,16,128]{0,2,1:T(8,128)(4,1)S(1)}, u32[]{:S(2)}) copy-start(pred[256,16,128]{0,2,1:T(8,128)(4,1)S(1)} %broadcast_in_dim.42) | copy-start | bytes 1572868
  81.3 4.0 %copy-start.1 = (f32[5,2048,256]{2,1,0:T(8,128)}, f32[5,2048,256]{2,1,0:T(8,128)S(1)}, u32[]{:S(2)}) copy-start(f32[5,2048,256]{2,1,0:T(8,128)S(1)} %get-tuple-element.13) | copy-start | bytes 31457284
  126.0 77.6 %reduce-scatter.8.cloned.1.call-start = ((), (), s32[]{:S(2)}) async-start(), calls=%async_computation.7 | async-start | bytes 2949120 | tf_op jit(solution)/shard_map/reduce_scatter | solution.py:152
  138.8 112.2 %reduce-scatter.6.cloned.1.call-start = ((), (), s32[]{:S(2)}) async-start(), calls=%async_computation.6 | async-start | bytes 2949120 | tf_op jit(solution)/shard_map/reduce_scatter | solution.py:146
  138.8 10.8 %copy-start.4 = (bf16[256,640]{0,1:T(8,128)(2,1)S(1)}, bf16[256,640]{0,1:T(8,128)(2,1)}, u32[]{:S(2)}) copy-start(bf16[256,640]{0,1:T(8,128)(2,1)} %copy.45) | copy-start | bytes 983044
  147.4 2.3 copy-start.2
Sparse Core Ops, SparseCore 0:
  9.6 34.9 all-gather.7
  47.1 29.9 all-gather.3
  78.9 30.1 all-gather.5
  126.1 31.2 reduce-scatter.9
  161.1 42.4 reduce-scatter.7
  207.4 43.6 reduce-scatter.5
where the time goes:
time: 259 us; the launch traced here: 258 us
  waiting for transfers between devices  156 us (60%)
  matrix products  43.4 us (17%)
  local copies, waits for them, and re-layouts  37.2 us (14%)
  between operations  14.2 us (5%)
  other arithmetic  6.45 us (2%)
    reduce_scatter x1, waiting for transfers between devices, per_device(): lax.psum_scatter(key_term.astype(jnp.float32).astype(jnp.bfloat16), 'ctx'...  47.4 us
    all_gather x1, waiting for transfers between devices, per_device(): full_cotangent = lax.all_gather(cotangent, 'head', axis=1, tiled=True)  30.2 us
    reduce_scatter x1, waiting for transfers between devices, per_device(): lax.psum_scatter(value_term.astype(jnp.float32).astype(jnp.bfloat16), 'ct...  28.6 us
    all_gather x1, waiting for transfers between devices, per_device(): lax.all_gather(keys, 'ctx', axis=0, tiled=True)  27.3 us
    all_gather x1, waiting for transfers between devices, per_device(): lax.all_gather(values, 'ctx', axis=0, tiled=True)  21.3 us
    unnamed x17, local copies, waits for them, and re-layouts  19 us
    dot_general x1, matrix products, step(): jnp.einsum('qhd,khd->qhk', g_three, v_three, preferred_element_type=jnp.f...  8.52 us
    dot_general x1, matrix products, step(): jnp.einsum('qhk,qhd->khd', probs.astype(jnp.bfloat16), g_three, preferred...  8.02 us
  transfers between devices with their start and end apart: 6, of which 5 were waited for; matrix products, arithmetic and copies ran while one was open for 25% of the time, Pallas kernels for 0%

commit v1 on v0

v1 whole, which is shorter than its diff:
```python
import functools
import math

import jax
import jax.numpy as jnp
from jax import lax
from jax.experimental import pallas as pl
from jax.experimental.pallas import tpu as pltpu
from jax.sharding import PartitionSpec as P

SIZE = 128
BLOCK = 128
NEG = -1e30
SCALE = SIZE ** (-0.5)
SCALE2 = SCALE * math.log2(math.e)
MESH = pl.DeviceIdType.MESH

NT = (((1,), (1,)), ((), ()))
TN = (((0,), (0,)), ((), ()))
NN = (((1,), (0,)), ((), ()))


def mm(a, b, dims):
    return lax.dot_general(a, b, dims, preferred_element_type=jnp.float32)


def kernel(
    chips, nhead, heads, unroll,
    bias, q, k, v, w, cot,
    mixed, qg, kg, vg,
    kv, probs, sbuf, att, att_t, inv, g_t, sib, rem, wbuf, cbuf, mstage, mrecv,
    lsem, wsem, clocal, gsend, grecv, csend, crecv, msend, mrsem, ssend, srecv, rsend, rrecv,
):
    rows = q.shape[0]
    width = heads * SIZE
    n = chips * 2
    bpr = rows // BLOCK
    me = lax.axis_index("ctx")
    mh = lax.axis_index("head")
    core = lax.rem(me, 2)
    chip = lax.div(me, 2)
    other = 1 - core
    sibling = chip * 2 + other
    mine = core * chips + chip

    def chip_at(d):
        return lax.rem(chip + d, chips)

    def head_at(d):
        return lax.rem(mh + d, nhead)

    def cols(h):
        return pl.ds(pl.multiple_of(h * SIZE, SIZE), SIZE)

    def remote(src, dst, ssem, rsem, where):
        return pltpu.make_async_remote_copy(
            src_ref=src, dst_ref=dst, send_sem=ssem, recv_sem=rsem,
            device_id=where, device_id_type=MESH,
        )

    def own_k(h):
        return pltpu.make_async_copy(k.at[:, cols(h)], kv.at[h, mine, 0], lsem.at[0, h])

    def own_v(h):
        return pltpu.make_async_copy(v.at[:, cols(h)], kv.at[h, mine, 1], lsem.at[1, h])

    def own_cot():
        return pltpu.make_async_copy(cot, cbuf.at[mh], clocal)

    def load_w(c):
        return pltpu.make_async_copy(
            w.at[:, pl.ds(c * width, width)], wbuf.at[c], wsem.at[c]
        )

    def direct(h, d):
        return remote(
            kv.at[h, mine], kv.at[h, mine], gsend.at[h, d - 1], grecv.at[h, mine],
            {"ctx": chip_at(d) * 2 + core},
        )

    def forward(h, d):
        slot = core * chips + chip_at(d)
        return remote(
            kv.at[h, slot], kv.at[h, slot], gsend.at[h, chips - 1 + d], grecv.at[h, slot],
            {"ctx": sibling},
        )

    def arrived(h, slot):
        return remote(
            kv.at[h, slot], kv.at[h, slot], gsend.at[h, 0], grecv.at[h, slot], {"ctx": sibling}
        )

    def cot_copy(d):
        return remote(
            cbuf.at[mh], cbuf.at[mh], csend.at[d - 1], crecv.at[mh], {"head": head_at(d)}
        )

    def cot_arrived(d):
        src = head_at(d)
        return remote(
            cbuf.at[src], cbuf.at[src], csend.at[d - 1], crecv.at[src], {"head": src}
        )

    def mixed_copy(d):
        return remote(
            mstage.at[d - 1], mrecv.at[d - 1], msend.at[d - 1], mrsem.at[d - 1],
            {"head": head_at(d)},
        )

    def sib_copy(h):
        return remote(
            kv.at[h, pl.ds(other * chips, chips)], sib.at[h], ssend.at[h], srecv.at[h],
            {"ctx": sibling},
        )

    def rem_copy(h, d):
        return remote(
            kv.at[h, core * chips + chip_at(d)], rem.at[h, d - 1],
            rsend.at[h, d - 1], rrecv.at[h, d - 1],
            {"ctx": chip_at(d) * 2 + core},
        )

    own_cot().start()

    @pl.loop(0, heads)
    def _(h):
        own_k(h).start()
        own_v(h).start()

    for c in range(nhead):
        load_w(c).start()

    barrier = pltpu.get_barrier_semaphore()
    for d in range(1, nhead):
        pl.semaphore_signal(barrier, inc=1, device_id={"head": head_at(d)}, device_id_type=MESH)
    for d in range(1, chips):
        pl.semaphore_signal(
            barrier, inc=1, device_id={"ctx": chip_at(d) * 2 + core}, device_id_type=MESH
        )
    pl.semaphore_signal(barrier, inc=1, device_id={"ctx": sibling}, device_id_type=MESH)
    pl.semaphore_wait(barrier, nhead - 1 + chips)

    own_cot().wait()
    for d in range(1, nhead):
        cot_copy(d).start()

    @pl.loop(0, heads)
    def _(h):
        own_k(h).wait()
        own_v(h).wait()
        for d in range(1, chips):
            direct(h, d).start()
        forward(h, 0).start()

    @pl.loop(0, heads)
    def _(h):
        for d in range(1, chips):
            arrived(h, core * chips + chip_at(d)).wait_recv()
            forward(h, d).start()
        for c in range(chips):
            arrived(h, other * chips + c).wait_recv()
        qh = q[:, cols(h)]

        def scores(i, best):
            s = mm(kv[h, i, 0], qh, NT)
            s = s.reshape(bpr, BLOCK, rows) + bias[i][:, None, :]
            s = s.reshape(rows, rows)
            sbuf[i] = s
            return jnp.maximum(best, jnp.max(s.reshape(rows // 8, 8, rows), axis=0))

        best = lax.fori_loop(
            0, n, scores, jnp.full((8, rows), 2 * NEG, jnp.float32), unroll=unroll
        )
        best = jnp.max(best, axis=0, keepdims=True)

        def weigh(i, carry):
            total, acc = carry
            p = jnp.exp2((sbuf[i] - best) * SCALE2)
            total = total + jnp.sum(p.reshape(rows // 8, 8, rows), axis=0)
            pb = p.astype(jnp.bfloat16)
            probs[h, i] = pb
            return total, acc + mm(kv[h, i, 1], pb, TN)

        total, acc = lax.fori_loop(
            0, n, weigh,
            (jnp.zeros((8, rows), jnp.float32), jnp.zeros((SIZE, rows), jnp.float32)),
            unroll=unroll,
        )
        scale = 1.0 / jnp.sum(total, axis=0, keepdims=True)
        inv[h] = scale
        out = acc * scale
        att_t[h] = out
        att[:, cols(h)] = out.T.astype(jnp.bfloat16)

    for c in range(nhead):
        load_w(c).wait()
    attended = att[...]
    for d in range(1, nhead):
        mstage[d - 1] = mm(attended, wbuf[head_at(d)], NN).astype(jnp.bfloat16)
        mixed_copy(d).start()

    g_t[...] = mm(wbuf[mh], cbuf[mh], NT)
    for d in range(1, nhead):
        cot_arrived(d).wait_recv()
        g_t[...] += mm(wbuf[head_at(d)], cbuf[head_at(d)], NT)

    def combine(h):
        sib_copy(h).wait_recv()
        for d in range(1, chips + 1):
            c = chip_at(d)
            slot = core * chips + c
            kv[h, slot] = (
                kv[h, slot].astype(jnp.float32) + sib[h, c].astype(jnp.float32)
            ).astype(jnp.bfloat16)
            if d < chips:
                rem_copy(h, d).start()

    @pl.loop(0, heads)
    def _(h):
        for d in range(1, chips):
            direct(h, d).wait_send()
        for d in range(chips):
            forward(h, d).wait_send()
        qh = q[:, cols(h)]
        at = att_t[h].astype(jnp.bfloat16).astype(jnp.float32)
        gt = g_t[pl.ds(pl.multiple_of(h * SIZE, SIZE), SIZE), :].astype(jnp.bfloat16)
        gt = gt.astype(jnp.float32) * inv[h]
        delta = jnp.sum(gt * at, axis=0, keepdims=True)
        gn = gt.T.astype(jnp.bfloat16)
        gt = gt.astype(jnp.bfloat16)

        def step(i, acc):
            kb, vb, pb = kv[h, i, 0], kv[h, i, 1], probs[h, i]
            dp = mm(vb, gt, NN)
            ds = (pb.astype(jnp.float32) * (dp - delta)).astype(jnp.bfloat16)
            kv[h, i, 0] = (mm(ds, qh, NN) * SCALE).astype(jnp.bfloat16)
            kv[h, i, 1] = mm(pb, gn, NN).astype(jnp.bfloat16)
            return acc + mm(kb, ds, TN)

        acc = lax.fori_loop(
            0, n, step, jnp.zeros((SIZE, rows), jnp.float32), unroll=unroll
        )
        qg[:, cols(h)] = (acc.T * SCALE).astype(jnp.bfloat16)
        sib_copy(h).start()

        @pl.when(h > 0)
        def _():
            combine(h - 1)

    combine(heads - 1)

    total = mm(attended, wbuf[mh], NN)
    for d in range(1, nhead):
        mixed_copy(d).wait_recv()
        total += mrecv[d - 1].astype(jnp.float32)
    mixed[...] = total.astype(jnp.bfloat16)

    @pl.loop(0, heads)
    def _(h):
        total = kv[h, mine].astype(jnp.float32)
        for d in range(1, chips):
            rem_copy(h, d).wait_recv()
            total += rem[h, d - 1].astype(jnp.float32)
        kg[:, cols(h)] = total[0].astype(jnp.bfloat16)
        vg[:, cols(h)] = total[1].astype(jnp.bfloat16)

    for d in range(1, nhead):
        cot_copy(d).wait_send()
        mixed_copy(d).wait_send()

    @pl.loop(0, heads)
    def _(h):
        sib_copy(h).wait_send()
        for d in range(1, chips):
            rem_copy(h, d).wait_send()


def per_device(queries, keys, values, out_weight, cotangent, contacts, chains):
    rows, width = queries.shape
    heads = width // SIZE
    n = lax.axis_size("ctx")
    nhead = lax.axis_size("head")
    chips = n // 2
    bpr = rows // BLOCK
    allowed = jnp.logical_or(chains[:, None] == chains[None, :], contacts > 0)
    own = lax.dynamic_slice(
        allowed, (lax.axis_index("ctx") * bpr, 0), (bpr, allowed.shape[1])
    )
    bias = jnp.where(own, 0.0, NEG).astype(jnp.float32)
    bias = bias.reshape(bpr, chips, 2, bpr).transpose(2, 1, 3, 0)
    bias = jnp.repeat(bias.reshape(n, bpr, bpr), BLOCK, axis=2)
    out = jax.ShapeDtypeStruct((rows, width), jnp.bfloat16)
    vmem = pl.BlockSpec(memory_space=pltpu.VMEM)
    hbm = pl.BlockSpec(memory_space=pl.ANY)
    bf16, f32 = jnp.bfloat16, jnp.float32
    dma = pltpu.SemaphoreType.DMA
    flops = 2 * rows * n * rows * width * 6 + 4 * rows * width * width * nhead
    return pl.pallas_call(
        functools.partial(kernel, chips, nhead, heads, 4),
        out_shape=(out, out, out, out),
        in_specs=[vmem, vmem, hbm, hbm, hbm, hbm],
        out_specs=(vmem, vmem, vmem, vmem),
        scratch_shapes=[
            pltpu.VMEM((heads, n, 2, rows, SIZE), bf16),
            pltpu.VMEM((heads, n, rows, rows), bf16),
            pltpu.VMEM((n, rows, rows), f32),
            pltpu.VMEM((rows, width), bf16),
            pltpu.VMEM((heads, SIZE, rows), f32),
            pltpu.VMEM((heads, 1, rows), f32),
            pltpu.VMEM((width, rows), f32),
            pltpu.VMEM((heads, chips, 2, rows, SIZE), bf16),
            pltpu.VMEM((heads, chips - 1, 2, rows, SIZE), bf16),
            pltpu.VMEM((nhead, width, width), bf16),
            pltpu.VMEM((nhead, rows, width), bf16),
            pltpu.VMEM((nhead - 1, rows, width), bf16),
            pltpu.VMEM((nhead - 1, rows, width), bf16),
            dma((2, heads)),
            dma((nhead,)),
            dma,
            dma((heads, 2 * chips - 1)),
            dma((heads, n)),
            dma((nhead - 1,)),
            dma((nhead,)),
            dma((nhead - 1,)),
            dma((nhead - 1,)),
            dma((heads,)),
            dma((heads,)),
            dma((heads, chips - 1)),
            dma((heads, chips - 1)),
        ],
        compiler_params=pltpu.CompilerParams(
            collective_id=0, has_side_effects=True, vmem_limit_bytes=60 * 2**20
        ),
        cost_estimate=pl.CostEstimate(
            flops=flops, bytes_accessed=16 * rows * width, transcendentals=rows * n * rows * heads
        ),
        name="attention",
    )(bias, queries, keys, values, out_weight, cotangent)


def solution(mesh):
    split = P("ctx", "head")
    return jax.shard_map(
        per_device,
        mesh=mesh,
        in_specs=(split, split, split, P("head", None), split, P(), P()),
        out_specs=(split, split, split, split),
        check_vma=False,
    )
```

time: 259 us -> 90.5 us (0.35)
  waiting for transfers between devices: 156 us -> 0 us
  Pallas kernels: 0 us -> 80.2 us
  matrix products: 43.4 us -> 0 us
  local copies, waits for them, and re-layouts: 37.2 us -> 8.57 us
  between operations: 14.2 us -> 0.65 us
  other arithmetic: 6.45 us -> 0.76 us
    pallas_call x0 -> x1, Pallas kernels: none -> 80.2 us  [per_device(): pl.pallas_call(functools.partial(kernel, chips, nhead, heads, 4), out_sha...]
    all_gather x3 -> x0, waiting for transfers between devices: 78.8 us -> none  [the longest x1 30.2 us: per_device(): full_cotangent = lax.all_gather(cotangent, 'head', axis=1, tiled=True)]
    reduce_scatter x2 -> x0, waiting for transfers between devices: 76 us -> none  [the longest x1 47.4 us: per_device(): lax.psum_scatter(key_term.astype(jnp.float32).astype(jnp.bfloat16), 'ctx'...]
    dot_general x8 -> x0, matrix products: 43.4 us -> none  [the longest x1 8.52 us: step(): jnp.einsum('qhd,khd->qhk', g_three, v_three, preferred_element_type=jnp.f...]
    unnamed x17 -> x4, local copies, waits for them, and re-layouts: 19 us -> 6.9 us
    reshape x2 -> x3, local copies, waits for them, and re-layouts: 8.9 us -> 0.87 us  [the longest x2 0.78 us: per_device(): bias = jnp.repeat(bias.reshape(n, bpr, bpr), BLOCK, axis=2)]
    reduce_sum x2 -> x0, other arithmetic: 5.67 us -> none  [the longest x1 3.16 us: step(): q_accum = jnp.sum(rounded(q_parts), axis=0)]
    all_gather x1 -> x0, local copies, waits for them, and re-layouts: 4.51 us -> none  [per_device(): lax.all_gather(values, 'ctx', axis=0, tiled=True)]
  transfers between devices with their start and end apart: 6 -> 0, of which waited for: 5 -> 0; matrix products, arithmetic and copies ran while one was open for 25% -> 0% of each run, Pallas kernels for 0% -> 0%
where the time goes in v1:
time: 90.5 us; the launch traced here: 90.2 us
  Pallas kernels  80.2 us (89%)
  local copies, waits for them, and re-layouts  8.57 us (9%)
    pallas_call x1, Pallas kernels, per_device(): pl.pallas_call(functools.partial(kernel, chips, nhead, heads, 4), out_sha...  80.2 us
    unnamed x4, local copies, waits for them, and re-layouts  6.9 us

profile of v1, /device:TPU:0, one launch (start us, length us, event | category | flops | bytes accessed | tf_op | source)
XLA Modules:
  0.0 90.2 jit_solution(9846239574232360637)
XLA Ops:
  0.6 0.7 dynamic-slice
  1.4 0.8 or_select_fusion
  2.1 0.1 reshape.19
  2.2 0.1 copy.15
  2.4 0.1 broadcast_in_dim.15
  2.4 0.6 reshape.21.bias
  3.1 80.2 %attention.1 = (bf16[256,640]{1,0:T(8,128)(2,1)}, bf16[256,640]{1,0:T(8,128)(2,1)}, bf16[256,640]{1,0:T(8,128)(2,1)}, bf16[256,640]{1,0:T(8,128)(2,1)}) custom-call(f32[8,2,256]{2,1,0:T(2,128)} %reshape.21.bias, bf16[256,640]{1,0:T(8,128)(2,1)} %q.1, bf16[256,640]{1,0:T(8,128)(2,1)} %k.1, bf16[256,640]{1,0:T(8,128)(2,1)} %v.1, bf16[640,2560]{1,0:T(8,128)(2,1)} %w.1, ...), custom_call_target="tpu_custom_call" | custom-call | flops 5704253440 | bytes 2621440 | tf_op jit(solution)/shard_map/attention/pallas_call | solution.py:298
  83.3 1.7 %copy.21 = bf16[256,640]{1,0:T(8,128)(2,1)} copy(bf16[256,640]{1,0:T(8,128)(2,1)} %get-tuple-element.8) | data formatting | bytes 655360
  85.0 1.7 %copy.22 = bf16[256,640]{1,0:T(8,128)(2,1)} copy(bf16[256,640]{1,0:T(8,128)(2,1)} %get-tuple-element.9) | data formatting | bytes 655360
  86.7 1.7 %copy.23 = bf16[256,640]{1,0:T(8,128)(2,1)} copy(bf16[256,640]{1,0:T(8,128)(2,1)} %get-tuple-element.10) | data formatting | bytes 655360
  88.4 1.7 %copy.24 = bf16[256,640]{1,0:T(8,128)(2,1)} copy(bf16[256,640]{1,0:T(8,128)(2,1)} %get-tuple-element.11) | data formatting | bytes 655360

commit v2 on v1

--- a/solution.py
+++ b/solution.py
@@ -26,9 +26,9 @@
 
 def kernel(
     chips, nhead, heads, unroll,
-    bias, q, k, v, w, cot,
+    chains, contacts, q, k, v, w, cot,
     mixed, qg, kg, vg,
-    kv, probs, sbuf, att, att_t, inv, g_t, sib, rem, wbuf, cbuf, mstage, mrecv,
+    bias, kv, probs, sbuf, att, att_t, inv, g_t, sib, rem, wbuf, cbuf, mstage, mrecv,
     lsem, wsem, clocal, gsend, grecv, csend, crecv, msend, mrsem, ssend, srecv, rsend, rrecv,
 ):
     rows = q.shape[0]
@@ -130,6 +130,19 @@
     for c in range(nhead):
         load_w(c).start()
 
+    for core_of in range(2):
+        for c in range(chips):
+            for b in range(bpr):
+                key_block = (c * 2 + core_of) * bpr + b
+                for a in range(bpr):
+                    query_block = me * bpr + a
+                    keep = (chains[query_block] == chains[key_block]) | (
+                        contacts[query_block, key_block] > 0
+                    )
+                    bias[core_of * chips + c, pl.ds(b, 1), pl.ds(a * BLOCK, BLOCK)] = jnp.full(
+                        (1, BLOCK), jnp.where(keep, 0.0, NEG), jnp.float32
+                    )
+
     barrier = pltpu.get_barrier_semaphore()
     for d in range(1, nhead):
         pl.semaphore_signal(barrier, inc=1, device_id={"head": head_at(d)}, device_id_type=MESH)
@@ -275,6 +288,23 @@
             rem_copy(h, d).wait_send()
 
 
+def hand_over(a, b, c, d, a_out, b_out, c_out, d_out, held, sems):
+    def taken(i, src):
+        return pltpu.make_async_copy(src, held.at[i], sems.at[0, i])
+
+    def given(i, dst):
+        return pltpu.make_async_copy(held.at[i], dst, sems.at[1, i])
+
+    sources, targets = (a, b, c, d), (a_out, b_out, c_out, d_out)
+    for i in range(4):
+        taken(i, sources[i]).start()
+    for i in range(4):
+        taken(i, sources[i]).wait()
+        given(i, targets[i]).start()
+    for i in range(4):
+        given(i, targets[i]).wait()
+
+
 def per_device(queries, keys, values, out_weight, cotangent, contacts, chains):
     rows, width = queries.shape
     heads = width // SIZE
@@ -282,25 +312,20 @@
     nhead = lax.axis_size("head")
     chips = n // 2
     bpr = rows // BLOCK
-    allowed = jnp.logical_or(chains[:, None] == chains[None, :], contacts > 0)
-    own = lax.dynamic_slice(
-        allowed, (lax.axis_index("ctx") * bpr, 0), (bpr, allowed.shape[1])
-    )
-    bias = jnp.where(own, 0.0, NEG).astype(jnp.float32)
-    bias = bias.reshape(bpr, chips, 2, bpr).transpose(2, 1, 3, 0)
-    bias = jnp.repeat(bias.reshape(n, bpr, bpr), BLOCK, axis=2)
     out = jax.ShapeDtypeStruct((rows, width), jnp.bfloat16)
     vmem = pl.BlockSpec(memory_space=pltpu.VMEM)
+    smem = pl.BlockSpec(memory_space=pltpu.SMEM)
     hbm = pl.BlockSpec(memory_space=pl.ANY)
     bf16, f32 = jnp.bfloat16, jnp.float32
     dma = pltpu.SemaphoreType.DMA
     flops = 2 * rows * n * rows * width * 6 + 4 * rows * width * width * nhead
-    return pl.pallas_call(
+    results = pl.pallas_call(
         functools.partial(kernel, chips, nhead, heads, 4),
         out_shape=(out, out, out, out),
-        in_specs=[vmem, vmem, hbm, hbm, hbm, hbm],
+        in_specs=[smem, smem, vmem, hbm, hbm, hbm, hbm],
         out_specs=(vmem, vmem, vmem, vmem),
         scratch_shapes=[
+            pltpu.VMEM((n, bpr, rows), f32),
             pltpu.VMEM((heads, n, 2, rows, SIZE), bf16),
             pltpu.VMEM((heads, n, rows, rows), bf16),
             pltpu.VMEM((n, rows, rows), f32),
@@ -335,7 +360,15 @@
             flops=flops, bytes_accessed=16 * rows * width, transcendentals=rows * n * rows * heads
         ),
         name="attention",
-    )(bias, queries, keys, values, out_weight, cotangent)
+    )(chains, contacts, queries, keys, values, out_weight, cotangent)
+    return pl.pallas_call(
+        hand_over,
+        out_shape=(out, out, out, out),
+        in_specs=[hbm] * 4,
+        out_specs=(hbm,) * 4,
+        scratch_shapes=[pltpu.VMEM((4, rows, width), bf16), dma((2, 4))],
+        name="hand_over",
+    )(*results)
 
 
 def solution(mesh):

time: 90.5 us -> 83.2 us (0.919)
  local copies, waits for them, and re-layouts: 8.57 us -> 0 us
  Pallas kernels: 80.2 us -> 82.4 us
    unnamed x4 -> x0, local copies, waits for them, and re-layouts: 6.9 us -> none
    pallas_call x0 -> x1, Pallas kernels: none -> 2.09 us  [per_device(): pl.pallas_call(hand_over, out_shape=(out, out, out, out), in_specs=[hbm]...]
where the time goes in v2:
time: 83.2 us; the launch traced here: 83.1 us
  Pallas kernels  82.4 us (99%)
    pallas_call x1, Pallas kernels, per_device(): pl.pallas_call(functools.partial(kernel, chips, nhead, heads, 4), out_sha...  80.3 us
    pallas_call x1, Pallas kernels, per_device(): pl.pallas_call(hand_over, out_shape=(out, out, out, out), in_specs=[hbm]...  2.09 us

profile of v2, /device:TPU:0, one launch (start us, length us, event | category | flops | bytes accessed | tf_op | source)
XLA Modules:
  0.0 83.1 jit_solution(18248057550311065028)
XLA Ops:
  0.6 80.3 %attention.1 = (bf16[256,640]{1,0:T(8,128)(2,1)}, bf16[256,640]{1,0:T(8,128)(2,1)}, bf16[256,640]{1,0:T(8,128)(2,1)}, bf16[256,640]{1,0:T(8,128)(2,1)}) custom-call(s32[16]{0:T(128)} %chains.1, s32[16,16]{1,0:T(8,128)} %contacts.1, bf16[256,640]{1,0:T(8,128)(2,1)} %q.1, bf16[256,640]{1,0:T(8,128)(2,1)} %k.1, bf16[256,640]{1,0:T(8,128)(2,1)} %v.1, ...), custom_call_target="tpu_custom_call" | custom-call | flops 5704253440 | bytes 2621440 | tf_op jit(solution)/shard_map/attention/pallas_call | solution.py:322
  81.0 2.1 %hand_over.1 = (bf16[256,640]{1,0:T(8,128)(2,1)}, bf16[256,640]{1,0:T(8,128)(2,1)}, bf16[256,640]{1,0:T(8,128)(2,1)}, bf16[256,640]{1,0:T(8,128)(2,1)}) custom-call(bf16[256,640]{1,0:T(8,128)(2,1)} %get-tuple-element.8.a, bf16[256,640]{1,0:T(8,128)(2,1)} %get-tuple-element.9.b, bf16[256,640]{1,0:T(8,128)(2,1)} %get-tuple-element.10.c, ...), custom_call_target="tpu_custom_call" | custom-call | tf_op jit(solution)/shard_map/hand_over/pallas_call | solution.py:364
